TPU v7x, 512 devices: a whole 4x8x8 slice. The times are simulated.
512 devices in a mesh: row: 32 (over y, z_hi), col: 16 (over z_lo, x, core).
Axes of the slice: x: 4, y: 8, z: 8 (z_hi: 4, z_lo: 2; z = z_hi * 2 + z_lo), core: 2. Of those that a mesh axis runs over, the one named last changes fastest.
Arguments:
- three_index: bfloat16 [32, 16, 8, 2, 128, 128], P('row', 'col'), may hold values from -6 to 6
- slot_pair: int32 [32, 16, 8], P('row', 'col'), may hold values from -1 to 31, as said below
- coeff: bfloat16 [16384, 256], P(('col', 'row')), may hold values from -0.125 to 0.125
- occ_mask: int32 [128, 2], P('col'), may hold values 0 or 1
Outputs:
- exchange_block: bfloat16 [16384, 16384], P('row', 'col')
Inputs may be any that keep to these rules, and one draw needn't show every extreme that they name: `slot_pair`: on each device (first two dimensions) the 8 slots name distinct local pair blocks mb * 8 + nb, the live ones first and -1 after them; in every draw some device fills all 8 slots.
All inputs are finite; a program needn't handle non-finite values. No bound on the sum of `occ_mask` on one device may be relied on, other than what follows from the above.
Results may differ from a plain program's by a relative error of at most 0.0057.
Values may be sent and summed in bfloat16 or wider, within the bound.
A program may use at most 64 MiB of HBM per device.

v0:
```python
import jax
import jax.numpy as jnp
from jax import lax
from jax.sharding import PartitionSpec as P

MB_DEV = 4


def spread(value, axis, root):
    mine = lax.axis_index(axis) == root
    return lax.psum(jnp.where(mine, value, jnp.zeros_like(value)), axis)


def body(three_index, slot_pair, coeff, occ_mask):
    block_size = three_index.shape[4]
    aux_count = three_index.shape[3]
    occ_count = coeff.shape[1]
    gathered = lax.all_gather(coeff, "row", axis=0, tiled=True)
    nu_blocks = gathered.shape[0] // block_size
    occ_blocks = occ_count // block_size
    keep = occ_mask.astype(jnp.bfloat16)[:, None, :, None]
    masked = (gathered.reshape(nu_blocks, block_size, occ_blocks, block_size) * keep).reshape(
        gathered.shape[0], occ_count
    )
    blocks = three_index[0, 0]
    slots = slot_pair[0, 0]
    mu_rows_count = MB_DEV * block_size
    live_count = jnp.sum((slots >= 0).astype(jnp.int32))

    def add_slot(slot_index, partial_value):
        pair = slots[slot_index]
        mu_start = pair // nu_blocks * block_size
        nu_start = pair % nu_blocks * block_size
        rows = lax.dynamic_slice_in_dim(masked, nu_start, block_size, 0)
        term = jnp.einsum(
            "pab,bi->api", blocks[slot_index], rows, preferred_element_type=jnp.float32
        )
        current = lax.dynamic_slice_in_dim(partial_value, mu_start, block_size, 0)
        return lax.dynamic_update_slice_in_dim(partial_value, current + term, mu_start, 0)

    partial_value = jnp.zeros((mu_rows_count, aux_count, occ_count), jnp.float32)
    partial_value = lax.fori_loop(0, live_count, add_slot, partial_value)
    ratio = lax.axis_size("row") // lax.axis_size("col")
    col_place = lax.axis_index("col")
    mu_half = lax.psum(partial_value, "col").astype(jnp.bfloat16)
    pieces = []
    for mirror in range(ratio):
        pieces.append(spread(mu_half, "row", ratio * col_place + mirror))
    nu_half = jnp.concatenate(pieces, 0)
    left = mu_half.reshape(mu_rows_count, aux_count * occ_count)
    right = nu_half.reshape(nu_half.shape[0], aux_count * occ_count)
    product = lax.dot_general(
        left, right, (((1,), (1,)), ((), ())), preferred_element_type=jnp.float32
    )
    return (product / jnp.sqrt(jnp.float32(aux_count * occ_count))).astype(jnp.bfloat16)


def solution(mesh):
    return jax.shard_map(
        body,
        mesh=mesh,
        in_specs=(
            P("row", "col", None, None, None, None),
            P("row", "col", None),
            P(("col", "row"), None),
            P("col", None),
        ),
        out_specs=P("row", "col"),
        check_vma=False,
    )
```

profile of v0, /device:TPU:6, one launch (start us, length us, event | category | flops | bytes accessed | tf_op | source)
XLA Modules:
  0.0 528.3 jit_solution(11992172012928057767)
XLA Ops:
  6.5 0.0 all-reduce.4.cloned.1.call-start
  6.5 1.4 fusion.10
  7.9 0.7 convert_element_type.13
  8.6 0.1 copy.7
  8.7 90.9 %all_gather.3 = bf16[1024,256]{1,0:T(8,128)(2,1)S(1)} all-gather(bf16[32,256]{1,0:T(8,128)(2,1)} %param.8), channel_id=1, replica_groups=mesh['row'=32,'col'=16] {'row'}, dimensions={0}, use_global_device_ids=true | all-gather | bytes 540672 | tf_op jit(solution)/shard_map/all_gather | solution.py:18
  99.6 0.3 mul.27
  100.0 0.0 copy-start
  100.0 0.1 bitcast_multiply_fusion.1
  100.1 0.1 broadcast_in_dim.4.clone
  100.1 0.5 copy-done
  100.6 5.6 %while.12 = (s32[]{:T(128)}, f32[512,2,256]{2,0,1:T(8,128)S(1)}, s32[]{:T(128)}, s32[8]{0:T(128)S(1)}, bf16[1024,256]{1,0:T(8,128)(2,1)S(1)}, /*index=5*/bf16[8,...) while((s32[]{:T(128)}, f32[512,2,256]{2,0,1:T(8,128)S(1)}, ...), condition=%wide.region_2.3_spmd, body=%wide.region_1.2_spmd.sunk | while | flops 16842784 | bytes 2753002 | solution.py:42
  101.3 0.6 dynamic_slice.40
  104.2 0.1 copy.18
  104.3 1.1 fusion.19
  105.4 0.1 copy.19
  106.3 85.8 %all-reduce.5 = bf16[512,2,256]{2,0,1:T(8,128)(2,1)S(1)} all-reduce(f32[512,2,256]{2,0,1:T(8,128)S(1)} %get-tuple-element.88), channel_id=1, replica_groups=mesh['row'=32,'col'=16] {'col'}, use_global_device_ids=true, to_apply=%region_3.4 | all-reduce | flops 262144 | bytes 1572864 | tf_op jit(solution)/shard_map/psum | solution.py:45
  192.1 1.1 broadcast_select_fusion.1
  193.2 0.0 all-reduce.4.cloned.1.call-update
  193.2 325.4 %all-reduce.4.cloned.1.call-done = (bf16[512,2,256]{2,0,1:T(8,128)(2,1)}, bf16[512,2,256]{2,0,1:T(8,128)(2,1)}) async-done(((bf16[512,2,256]{2,0,1:T(8,128)(2,1)}, bf16[512,2,256]{2,0,1:T(8,128)(2,1)}), (bf16[512,2,256]{2,0,1:T(8,128)(2,1)}, bf16[512,2,256]{2,0,1:T(8,128)(2,1)})) %all-reduce.4.cloned.1.call-update) | async-done | bytes 1048592 | tf_op jit(solution)/shard_map/psum | solution.py:11
  518.6 2.9 fusion.6
  (2 shorter events, 0.0 us)
Async XLA Ops:
  6.5 512.0 %all-reduce.4.cloned.1.call-start = ((), (), s32[]{:S(2)}) async-start(), calls=%async_computation | async-start | bytes 2097152 | tf_op jit(solution)/shard_map/psum | solution.py:11
  100.0 0.7 copy-start
Sparse Core Ops, SparseCore 0:
  193.3 325.1 all-reduce.3
where the time goes:
time: 528 us
  waiting for transfers between devices  325 us (62%)
  blocking collectives  177 us (34%)
  between operations  13.4 us (3%)
    psum x1, waiting for transfers between devices, spread(): return lax.psum(jnp.where(mine, value, jnp.zeros_like(value)), axis)  325 us
    all_gather x1, blocking collectives, body(): gathered = lax.all_gather(coeff, 'row', axis=0, tiled=True)  90.9 us
    psum x1, blocking collectives, body(): mu_half = lax.psum(partial_value, 'col').astype(jnp.bfloat16)  85.8 us
  transfers between devices with their start and end apart: 1, of which 1 were waited for; matrix products, arithmetic and copies ran while one was open for 0% of the time, Pallas kernels for 0%

commit v1 on v0

v1 whole, which is shorter than its diff:
```python
import jax
import jax.numpy as jnp
from jax import lax
from jax.experimental import pallas as pl
from jax.experimental.pallas import tpu as pltpu
from jax.sharding import PartitionSpec as P

MESH = pl.DeviceIdType.MESH
BF16 = jnp.bfloat16
F32 = jnp.float32
NY, NZH, NX = 8, 4, 4
Y_ORDER = (4, 3, 5, 2, 6, 1, 7)
Z_ORDER = (2, 1, 3)
SCALE = 512.0**-0.5


def kernel(
    slot_ref, mask_ref, coeff_ref, blocks_ref, out_ref,
    blocks, ga, gb, rhs, part, own, theirs, summed, landed, piece, mu, ya, zb, nua, nub, sends, recvs, local,
):
    row, col = lax.axis_index("row"), lax.axis_index("col")
    y, zh = row // NZH, row % NZH
    chip, k = col // 2, col % 2
    zl, x = chip // NX, chip % NX

    def along_y(d):
        return (((y + d) % NY) * NZH + zh, col)

    def along_z(d):
        return (y * NZH + (zh + d) % NZH, col)

    def in_row(d):
        return (row, ((chip + d) % 8) * 2 + k)

    sibling = (row, chip * 2 + 1 - k)

    def send(src, dst, index, device):
        pltpu.make_async_remote_copy(
            src_ref=src, dst_ref=dst, send_sem=sends.at[index], recv_sem=recvs.at[index],
            device_id=device, device_id_type=MESH,
        ).start()

    def took(sems, index, ref):
        pltpu.make_async_copy(ref, ref, sems.at[index]).wait()

    fetch = pltpu.make_async_copy(blocks_ref, blocks, local)
    fetch.start()
    ga[y, zh] = coeff_ref[:, 0:128]
    gb[zh, y] = coeff_ref[:, 128:256]

    barrier = pltpu.get_barrier_semaphore()
    peers = [along_y(d) for d in Y_ORDER] + [along_z(d) for d in Z_ORDER] + [in_row(d) for d in range(1, 8)] + [sibling]
    for peer in peers:
        pl.semaphore_signal(barrier, inc=1, device_id=peer, device_id_type=MESH)
    pl.semaphore_wait(barrier, len(peers))

    for d in Z_ORDER:
        send(ga.at[y, zh], ga.at[y, zh], 0, along_z(d))
    for d in Y_ORDER:
        send(gb.at[zh, y], gb.at[zh, y], 1, along_y(d))
    took(recvs, 0, ga.at[0, pl.ds(0, 3)])
    for d in Y_ORDER:
        send(ga.at[y], ga.at[y], 2, along_y(d))
    took(recvs, 1, gb.at[0, pl.ds(0, 7)])
    for d in Z_ORDER:
        send(gb.at[zh], gb.at[zh], 3, along_z(d))
    fetch.wait()
    took(recvs, 2, ga.at[pl.ds(0, 7)])
    took(recvs, 3, gb.at[pl.ds(0, 3)])

    zeros = jnp.zeros((128, 128), BF16)
    for s in range(8):
        nb = slot_ref[0, 0, s] & 7
        rows = pl.ds(s * 128, 128)
        rhs[rows, 0:128] = jnp.where(mask_ref[nb, 0] != 0, ga[nb].reshape(128, 128), zeros)
        rhs[rows, 128:256] = jnp.where(mask_ref[nb, 1] != 0, gb[:, nb].reshape(128, 128), zeros)

    def partial(mb):
        zero = jnp.zeros((256, 128), BF16)
        lhs = [
            jnp.where((slot_ref[0, 0, s] >> 3) == mb, blocks[s].reshape(256, 128), zero)
            for s in range(8)
        ]
        return jnp.dot(jnp.concatenate(lhs, axis=1), rhs[...], preferred_element_type=F32)

    for j in range(2):
        value = partial((1 - k) * 2 + j).astype(BF16)
        for p in range(2):
            part[pl.ds(j * 128, 128), p * 256 : (p + 1) * 256] = value[p * 128 : (p + 1) * 128]
    send(part, theirs, 4, sibling)
    for j in range(2):
        value = partial(k * 2 + j)
        for p in range(2):
            own[pl.ds(j * 128, 128), p * 256 : (p + 1) * 256] = value[p * 128 : (p + 1) * 128]
    took(recvs, 4, theirs)
    total = own[...] + theirs[...].astype(F32)
    own[...] = total
    summed[...] = total.astype(BF16).reshape(8, 32, 512)
    for d in (6, 2, 5, 7, 1, 3, 4):
        send(summed.at[(chip + d) % 8], landed.at[chip], 5, in_row(d))
    landed[chip] = jnp.zeros((32, 512), BF16)
    took(recvs, 5, landed.at[pl.ds(0, 7)])
    total = own[pl.ds(chip * 32, 32), :]
    for m in range(8):
        total = total + landed[m].astype(F32)
    total = total.astype(BF16)
    place = k * 8 + chip
    for p in range(2):
        piece[p] = total[:, p * 256 : (p + 1) * 256]
    ya[y] = piece[0]
    zb[zh] = piece[1]
    for p in range(2):
        mu[p, place] = piece[p]

    for d in Y_ORDER:
        send(ya.at[y], ya.at[y], 6, along_y(d))
    for d in Z_ORDER:
        send(zb.at[zh], zb.at[zh], 7, along_z(d))
    for d in (6, 2, 5, 7, 1, 3, 4):
        send(piece, mu.at[:, place], 8, in_row(d))
    took(recvs, 7, zb.at[pl.ds(0, 3)])
    at_home = chip == y
    for j in range(NY):
        yy = (y + 4 + j) % NY
        for kk in range(2):
            kt = (k + 1 + kk) % 2
            src, dst = zb.at[pl.ds(kt * 2, 2)], nub.at[:, place]
            target = (yy * NZH + zh, y * 2 + kt)
            if j == 4 and kk == 1:

                @pl.when(at_home)
                def _():
                    pltpu.make_async_copy(src, dst, recvs.at[9]).start()

                @pl.when(jnp.logical_not(at_home))
                def _():
                    send(src, dst, 9, target)
            else:
                send(src, dst, 9, target)
    took(recvs, 6, ya.at[pl.ds(0, 7)])
    same_core = k == zh // 2
    for j in range(NY):
        yp = (chip + 1 + j) % NY
        for d in (2, 1, 3, 0):
            src, dst = ya.at[yp], nua.at[zh % 2, place]
            target = (y * NZH + (zh + d) % NZH, yp * 2 + zh // 2)
            if j == 7 and d == 0:

                @pl.when(same_core)
                def _():
                    pltpu.make_async_copy(src, dst, recvs.at[10]).start()

                @pl.when(jnp.logical_not(same_core))
                def _():
                    send(src, dst, 10, target)
            else:
                send(src, dst, 10, target)
    took(recvs, 8, mu.at[:, pl.ds(0, 7)])
    half = mu.at[:, pl.ds(k * 8, 8)]
    send(half, half, 11, sibling)
    took(recvs, 11, mu.at[:, pl.ds(0, 8)])
    took(recvs, 9, nub)
    took(recvs, 10, nua)

    def dot(left, right):
        return lax.dot_general(left, right, (((1,), (1,)), ((), ())), preferred_element_type=F32)

    for h in range(2):
        for q in range(2):
            right = pl.ds(q * 8, 8)
            value = dot(mu[0].reshape(512, 256), nua[h, right].reshape(256, 256))
            value = value + dot(mu[1].reshape(512, 256), nub[h, right].reshape(256, 256))
            out_ref[:, h * 512 + q * 256 : h * 512 + (q + 1) * 256] = (value * SCALE).astype(BF16)

    took(sends, 0, ga.at[0, pl.ds(0, 3)])
    took(sends, 1, gb.at[0, pl.ds(0, 7)])
    took(sends, 2, ga.at[pl.ds(0, 7)])
    took(sends, 3, gb.at[pl.ds(0, 3)])
    took(sends, 4, theirs)
    took(sends, 5, landed.at[pl.ds(0, 7)])
    took(sends, 6, ya.at[pl.ds(0, 7)])
    took(sends, 7, zb.at[pl.ds(0, 3)])
    took(sends, 8, mu.at[:, pl.ds(0, 7)])
    took(sends, 11, mu.at[:, pl.ds(0, 8)])

    @pl.when(at_home)
    def _():
        took(sends, 9, nub.at[:, pl.ds(0, 15)])

    @pl.when(jnp.logical_not(at_home))
    def _():
        took(sends, 9, nub)

    @pl.when(same_core)
    def _():
        took(sends, 10, nua.at[0, pl.ds(0, 15)])
        took(sends, 10, nua.at[0])

    @pl.when(jnp.logical_not(same_core))
    def _():
        took(sends, 10, nua)


def body(three_index, slot_pair, coeff, occ_mask):
    return pl.pallas_call(
        kernel,
        out_shape=jax.ShapeDtypeStruct((512, 1024), BF16),
        in_specs=[
            pl.BlockSpec(memory_space=pltpu.SMEM),
            pl.BlockSpec(memory_space=pltpu.SMEM),
            pl.BlockSpec(memory_space=pltpu.VMEM),
            pl.BlockSpec(memory_space=pl.ANY),
        ],
        out_specs=pl.BlockSpec(memory_space=pltpu.VMEM),
        scratch_shapes=[
            pltpu.VMEM((8, 2, 128, 128), BF16),
            pltpu.VMEM((8, 4, 32, 128), BF16),
            pltpu.VMEM((4, 8, 32, 128), BF16),
            pltpu.VMEM((1024, 256), BF16),
            pltpu.VMEM((256, 512), BF16),
            pltpu.VMEM((256, 512), F32),
            pltpu.VMEM((256, 512), BF16),
            pltpu.VMEM((8, 32, 512), BF16),
            pltpu.VMEM((8, 32, 512), BF16),
            pltpu.VMEM((2, 32, 256), BF16),
            pltpu.VMEM((2, 16, 32, 256), BF16),
            pltpu.VMEM((8, 32, 256), BF16),
            pltpu.VMEM((4, 32, 256), BF16),
            pltpu.VMEM((2, 16, 32, 256), BF16),
            pltpu.VMEM((2, 16, 32, 256), BF16),
            pltpu.SemaphoreType.DMA((12,)),
            pltpu.SemaphoreType.DMA((12,)),
            pltpu.SemaphoreType.DMA,
        ],
        compiler_params=pltpu.CompilerParams(
            collective_id=0, has_side_effects=True, vmem_limit_bytes=40 * 2**20
        ),
        cost_estimate=pl.CostEstimate(flops=805306368, bytes_accessed=1638400, transcendentals=0),
    )(slot_pair, occ_mask, coeff, three_index.reshape(8, 2, 128, 128))


def solution(mesh):
    return jax.shard_map(
        body,
        mesh=mesh,
        in_specs=(
            P("row", "col", None, None, None, None),
            P("row", "col", None),
            P(("col", "row"), None),
            P("col", None),
        ),
        out_specs=P("row", "col"),
        check_vma=False,
    )
```

time: 528 us -> 65.4 us (0.12)
  the two profiles are of different devices: /device:TPU:6 before, /device:TPU:1 now
where the time goes in v1:
time: 65.4 us; the launch traced here: 65.1 us
  Pallas kernels  61 us (93%)
  local copies, waits for them, and re-layouts  4.06 us (6%)
    pallas_call x1, Pallas kernels, body(): pl.pallas_call(kernel, out_shape=jax.ShapeDtypeStruct((512, 1024), BF16),...  61 us
    unnamed x10, local copies, waits for them, and re-layouts  4.06 us

profile of v1, /device:TPU:1, one launch (start us, length us, event | category | flops | bytes accessed | tf_op | source)
XLA Modules:
  0.0 65.1 jit_solution(2162373780181528384)
XLA Ops:
  0.0 0.0 copy-start.3
  0.0 0.7 %copy-done.3 = s32[8,2]{0,1:T(2,128)S(1)} copy-done((s32[8,2]{0,1:T(2,128)S(1)}, s32[8,2]{0,1:T(2,128)}, u32[]{:S(2)}) %copy-start.3) | copy-done | bytes 88
  0.7 0.0 copy-start.2
  0.7 0.1 copy.5.mask_ref
  0.8 0.6 copy-done.2
  1.3 0.0 copy-start
  1.3 1.0 %copy-done = bf16[1,1,8,2,128,128]{5,4,3,2,1,0:T(8,128)(2,1)S(1)} copy-done((bf16[1,1,8,2,128,128]{5,4,3,2,1,0:T(8,128)(2,1)S(1)}, bf16[1,1,8,2,128,128]{5,4,3,2,1,0:T(8,128)(2,1)}, u32[]{:S(2)}) %copy-start) | copy-done | bytes 524312
  2.4 0.0 copy-start.1
  2.4 0.7 %copy-done.1 = bf16[32,256]{1,0:T(8,128)(2,1)S(1)} copy-done((bf16[32,256]{1,0:T(8,128)(2,1)S(1)}, bf16[32,256]{1,0:T(8,128)(2,1)}, u32[]{:S(2)}) %copy-start.1) | copy-done | bytes 16408
  3.1 61.0 %shard_map.46 = bf16[512,1024]{1,0:T(8,128)(2,1)S(1)} custom-call(s32[1,1,8]{2,1,0:T(1,128)S(1)} %copy-done.2, s32[8,2]{1,0:T(8,128)S(1)} %copy.5.mask_ref, bf16[32,256]{1,0:T(8,128)(2,1)S(1)} %copy-done.1, bf16[8,2,128,128]{3,2,1,0:T(8,128)(2,1)S(1)} %bitcast.1), custom_call_target="tpu_custom_call" | custom-call | flops 805306368 | bytes 1638400 | tf_op jit(solution)/shard_map/pallas_call | solution.py:205
  64.1 1.0 %copy.7 = bf16[512,1024]{1,0:T(8,128)(2,1)} copy(bf16[512,1024]{1,0:T(8,128)(2,1)S(1)} %shard_map.46) | data formatting | bytes 2097152
Async XLA Ops:
  0.0 0.7 %copy-start.3 = (s32[8,2]{0,1:T(2,128)S(1)}, s32[8,2]{0,1:T(2,128)}, u32[]{:S(2)}) copy-start(s32[8,2]{0,1:T(2,128)} %param.7) | copy-start | bytes 196
  0.7 0.7 %copy-start.2 = (s32[1,1,8]{2,1,0:T(1,128)S(1)}, s32[1,1,8]{2,1,0:T(1,128)}, u32[]{:S(2)}) copy-start(s32[1,1,8]{2,1,0:T(1,128)} %slot_ref.1) | copy-start | bytes 100
  1.3 1.0 %copy-start = (bf16[1,1,8,2,128,128]{5,4,3,2,1,0:T(8,128)(2,1)S(1)}, bf16[1,1,8,2,128,128]{5,4,3,2,1,0:T(8,128)(2,1)}, u32[]{:S(2)}) copy-start(bf16[1,1,8,2,128,128]{5,4,3,2,1,0:T(8,128)(2,1)} %param.4) | copy-start | bytes 1572868
  2.4 0.7 %copy-start.1 = (bf16[32,256]{1,0:T(8,128)(2,1)S(1)}, bf16[32,256]{1,0:T(8,128)(2,1)}, u32[]{:S(2)}) copy-start(bf16[32,256]{1,0:T(8,128)(2,1)} %coeff_ref.1) | copy-start | bytes 49156

commit v2 on v1

--- a/solution.py
+++ b/solution.py
@@ -15,8 +15,9 @@
 
 
 def kernel(
-    slot_ref, mask_ref, coeff_ref, blocks_ref, out_ref,
-    blocks, ga, gb, rhs, part, own, theirs, summed, landed, piece, mu, ya, zb, nua, nub, sends, recvs, local,
+    slot_hbm, mask_hbm, coeff_hbm, blocks_hbm, out_ref,
+    slot_ref, mask_ref, coeff_ref, blocks,
+    ga, gb, rhs, part, own, theirs, summed, landed, piece, mu, ya, zb, nua, nub, sends, recvs, local,
 ):
     row, col = lax.axis_index("row"), lax.axis_index("col")
     y, zh = row // NZH, row % NZH
@@ -43,15 +44,21 @@
     def took(sems, index, ref):
         pltpu.make_async_copy(ref, ref, sems.at[index]).wait()
 
-    fetch = pltpu.make_async_copy(blocks_ref, blocks, local)
-    fetch.start()
-    ga[y, zh] = coeff_ref[:, 0:128]
-    gb[zh, y] = coeff_ref[:, 128:256]
-
+    fetches = [
+        pltpu.make_async_copy(src, dst, local.at[n])
+        for n, (src, dst) in enumerate(
+            ((coeff_hbm, coeff_ref), (slot_hbm, slot_ref), (mask_hbm, mask_ref), (blocks_hbm, blocks))
+        )
+    ]
+    for fetch in fetches:
+        fetch.start()
     barrier = pltpu.get_barrier_semaphore()
     peers = [along_y(d) for d in Y_ORDER] + [along_z(d) for d in Z_ORDER] + [in_row(d) for d in range(1, 8)] + [sibling]
     for peer in peers:
         pl.semaphore_signal(barrier, inc=1, device_id=peer, device_id_type=MESH)
+    fetches[0].wait()
+    ga[y, zh] = coeff_ref[:, 0:128]
+    gb[zh, y] = coeff_ref[:, 128:256]
     pl.semaphore_wait(barrier, len(peers))
 
     for d in Z_ORDER:
@@ -64,7 +71,8 @@
     took(recvs, 1, gb.at[0, pl.ds(0, 7)])
     for d in Z_ORDER:
         send(gb.at[zh], gb.at[zh], 3, along_z(d))
-    fetch.wait()
+    for fetch in fetches[1:]:
+        fetch.wait()
     took(recvs, 2, ga.at[pl.ds(0, 7)])
     took(recvs, 3, gb.at[pl.ds(0, 3)])
 
@@ -72,8 +80,8 @@
     for s in range(8):
         nb = slot_ref[0, 0, s] & 7
         rows = pl.ds(s * 128, 128)
-        rhs[rows, 0:128] = jnp.where(mask_ref[nb, 0] != 0, ga[nb].reshape(128, 128), zeros)
-        rhs[rows, 128:256] = jnp.where(mask_ref[nb, 1] != 0, gb[:, nb].reshape(128, 128), zeros)
+        rhs[rows, 0:128] = jnp.where(mask_ref[0, nb] != 0, ga[nb].reshape(128, 128), zeros)
+        rhs[rows, 128:256] = jnp.where(mask_ref[1, nb] != 0, gb[:, nb].reshape(128, 128), zeros)
 
     def partial(mb):
         zero = jnp.zeros((256, 128), BF16)
@@ -105,12 +113,14 @@
         total = total + landed[m].astype(F32)
     total = total.astype(BF16)
     place = k * 8 + chip
-    for p in range(2):
-        piece[p] = total[:, p * 256 : (p + 1) * 256]
-    ya[y] = piece[0]
-    zb[zh] = piece[1]
-    for p in range(2):
-        mu[p, place] = piece[p]
+    for q in range(4):
+        block = total[:, q * 128 : (q + 1) * 128]
+        piece[q] = block
+        mu[q, place] = block
+        if q == 0:
+            ya[y] = block
+        else:
+            zb[zh, q - 1] = block
 
     for d in Y_ORDER:
         send(ya.at[y], ya.at[y], 6, along_y(d))
@@ -124,7 +134,7 @@
         yy = (y + 4 + j) % NY
         for kk in range(2):
             kt = (k + 1 + kk) % 2
-            src, dst = zb.at[pl.ds(kt * 2, 2)], nub.at[:, place]
+            src, dst = zb.at[pl.ds(kt * 2, 2)], nub.at[:, :, place]
             target = (yy * NZH + zh, y * 2 + kt)
             if j == 4 and kk == 1:
 
@@ -165,12 +175,13 @@
     def dot(left, right):
         return lax.dot_general(left, right, (((1,), (1,)), ((), ())), preferred_element_type=F32)
 
+    left = jnp.concatenate([mu[q].reshape(512, 128) for q in range(4)], axis=1)
     for h in range(2):
-        for q in range(2):
-            right = pl.ds(q * 8, 8)
-            value = dot(mu[0].reshape(512, 256), nua[h, right].reshape(256, 256))
-            value = value + dot(mu[1].reshape(512, 256), nub[h, right].reshape(256, 256))
-            out_ref[:, h * 512 + q * 256 : h * 512 + (q + 1) * 256] = (value * SCALE).astype(BF16)
+        for n in range(2):
+            at = pl.ds(n * 8, 8)
+            right = [nua[h, at]] + [nub[h, q, at] for q in range(3)]
+            value = dot(left, jnp.concatenate([v.reshape(256, 128) for v in right], axis=1))
+            out_ref[:, h * 512 + n * 256 : h * 512 + (n + 1) * 256] = (value * SCALE).astype(BF16)
 
     took(sends, 0, ga.at[0, pl.ds(0, 3)])
     took(sends, 1, gb.at[0, pl.ds(0, 7)])
@@ -185,7 +196,7 @@
 
     @pl.when(at_home)
     def _():
-        took(sends, 9, nub.at[:, pl.ds(0, 15)])
+        took(sends, 9, nub.at[:, :, pl.ds(0, 15)])
 
     @pl.when(jnp.logical_not(at_home))
     def _():
@@ -202,17 +213,21 @@
 
 
 def body(three_index, slot_pair, coeff, occ_mask):
+    arrays = (slot_pair, occ_mask.T, coeff, three_index.reshape(8, 2, 128, 128))
     return pl.pallas_call(
         kernel,
         out_shape=jax.ShapeDtypeStruct((512, 1024), BF16),
         in_specs=[
-            pl.BlockSpec(memory_space=pltpu.SMEM),
-            pl.BlockSpec(memory_space=pltpu.SMEM),
-            pl.BlockSpec(memory_space=pltpu.VMEM),
-            pl.BlockSpec(memory_space=pl.ANY),
+            pl.BlockSpec(memory_space=pltpu.HBM),
+            pl.BlockSpec(memory_space=pltpu.HBM),
+            pl.BlockSpec(memory_space=pltpu.HBM),
+            pl.BlockSpec(memory_space=pltpu.HBM),
         ],
         out_specs=pl.BlockSpec(memory_space=pltpu.VMEM),
         scratch_shapes=[
+            pltpu.SMEM((1, 1, 8), jnp.int32),
+            pltpu.SMEM((2, 8), jnp.int32),
+            pltpu.VMEM((32, 256), BF16),
             pltpu.VMEM((8, 2, 128, 128), BF16),
             pltpu.VMEM((8, 4, 32, 128), BF16),
             pltpu.VMEM((4, 8, 32, 128), BF16),
@@ -222,21 +237,21 @@
             pltpu.VMEM((256, 512), BF16),
             pltpu.VMEM((8, 32, 512), BF16),
             pltpu.VMEM((8, 32, 512), BF16),
-            pltpu.VMEM((2, 32, 256), BF16),
-            pltpu.VMEM((2, 16, 32, 256), BF16),
-            pltpu.VMEM((8, 32, 256), BF16),
-            pltpu.VMEM((4, 32, 256), BF16),
-            pltpu.VMEM((2, 16, 32, 256), BF16),
-            pltpu.VMEM((2, 16, 32, 256), BF16),
+            pltpu.VMEM((4, 32, 128), BF16),
+            pltpu.VMEM((4, 16, 32, 128), BF16),
+            pltpu.VMEM((8, 32, 128), BF16),
+            pltpu.VMEM((4, 3, 32, 128), BF16),
+            pltpu.VMEM((2, 16, 32, 128), BF16),
+            pltpu.VMEM((2, 3, 16, 32, 128), BF16),
             pltpu.SemaphoreType.DMA((12,)),
             pltpu.SemaphoreType.DMA((12,)),
-            pltpu.SemaphoreType.DMA,
+            pltpu.SemaphoreType.DMA((4,)),
         ],
         compiler_params=pltpu.CompilerParams(
             collective_id=0, has_side_effects=True, vmem_limit_bytes=40 * 2**20
         ),
         cost_estimate=pl.CostEstimate(flops=805306368, bytes_accessed=1638400, transcendentals=0),
-    )(slot_pair, occ_mask, coeff, three_index.reshape(8, 2, 128, 128))
+    )(*(pltpu.with_memory_space_constraint(v, pltpu.HBM) for v in arrays))
 
 
 def solution(mesh):

time: 65.4 us -> 63.8 us (0.976); the launches traced: 65.1 us -> 62.6 us
  local copies, waits for them, and re-layouts: 4.06 us -> 0.97 us
    unnamed x10 -> x1, local copies, waits for them, and re-layouts: 4.06 us -> 0.97 us
where the time goes in v2:
time: 63.8 us; the launch traced here: 62.6 us
  Pallas kernels  61.6 us (97%)
  local copies, waits for them, and re-layouts  0.97 us (2%)
    pallas_call x1, Pallas kernels, body(): pl.pallas_call(kernel, out_shape=jax.ShapeDtypeStruct((512, 1024), BF16),...  61.6 us

profile of v2, /device:TPU:1, one launch (start us, length us, event | category | flops | bytes accessed | tf_op | source)
XLA Modules:
  0.0 62.6 jit_solution(17509781781797927004)
XLA Ops:
  0.0 61.6 %shard_map.46 = bf16[512,1024]{1,0:T(8,128)(2,1)S(1)} custom-call(s32[1,1,8]{2,1,0:T(1,128)} %slot_hbm.1, s32[2,8]{1,0:T(2,128)} %bitcast.3, bf16[32,256]{1,0:T(8,128)(2,1)} %coeff_hbm.1, bf16[8,2,128,128]{3,2,1,0:T(8,128)(2,1)} %bitcast.2), custom_call_target="tpu_custom_call" | custom-call | flops 805306368 | bytes 1638400 | tf_op jit(solution)/shard_map/pallas_call | solution.py:217
  61.6 1.0 %copy.6 = bf16[512,1024]{1,0:T(8,128)(2,1)} copy(bf16[512,1024]{1,0:T(8,128)(2,1)S(1)} %shard_map.46) | data formatting | bytes 2097152

commit v3 on v2

--- a/solution.py
+++ b/solution.py
@@ -11,6 +11,8 @@
 NY, NZH, NX = 8, 4, 4
 Y_ORDER = (4, 3, 5, 2, 6, 1, 7)
 Z_ORDER = (2, 1, 3)
+A_ORDER_P = (6, 1, 3, 2, 5, 7, 4, 0)
+A_ORDER_Z = (2, 1, 3, 0)
 SCALE = 512.0**-0.5
 
 
@@ -117,59 +119,48 @@
         block = total[:, q * 128 : (q + 1) * 128]
         piece[q] = block
         mu[q, place] = block
-        if q == 0:
-            ya[y] = block
-        else:
-            zb[zh, q - 1] = block
-
+        if q < 2:
+            ya[y, q] = block
+
+    at_home, same_core = chip == y, k == zh // 2
+
+    def deliver(src, dst, index, device, here):
+        if here is None:
+            send(src, dst, index, device)
+            return
+
+        @pl.when(here)
+        def _():
+            pltpu.make_async_copy(src, dst, recvs.at[index]).start()
+
+        @pl.when(jnp.logical_not(here))
+        def _():
+            send(src, dst, index, device)
+
+    late = piece.at[pl.ds(2, 2)]
+    for dz in (2, 1, 3, 0):
+        target = (chip * NZH + (zh + dz) % NZH, y * 2 + zh // 2)
+        deliver(late, zb.at[zh % 2, :, k], 7, target, at_home & same_core if dz == 0 else None)
     for d in Y_ORDER:
         send(ya.at[y], ya.at[y], 6, along_y(d))
-    for d in Z_ORDER:
-        send(zb.at[zh], zb.at[zh], 7, along_z(d))
     for d in (6, 2, 5, 7, 1, 3, 4):
         send(piece, mu.at[:, place], 8, in_row(d))
-    took(recvs, 7, zb.at[pl.ds(0, 3)])
-    at_home = chip == y
-    for j in range(NY):
-        yy = (y + 4 + j) % NY
-        for kk in range(2):
-            kt = (k + 1 + kk) % 2
-            src, dst = zb.at[pl.ds(kt * 2, 2)], nub.at[:, :, place]
-            target = (yy * NZH + zh, y * 2 + kt)
-            if j == 4 and kk == 1:
-
-                @pl.when(at_home)
-                def _():
-                    pltpu.make_async_copy(src, dst, recvs.at[9]).start()
-
-                @pl.when(jnp.logical_not(at_home))
-                def _():
-                    send(src, dst, 9, target)
-            else:
-                send(src, dst, 9, target)
     took(recvs, 6, ya.at[pl.ds(0, 7)])
-    same_core = k == zh // 2
-    for j in range(NY):
-        yp = (chip + 1 + j) % NY
-        for d in (2, 1, 3, 0):
-            src, dst = ya.at[yp], nua.at[zh % 2, place]
-            target = (y * NZH + (zh + d) % NZH, yp * 2 + zh // 2)
-            if j == 7 and d == 0:
-
-                @pl.when(same_core)
-                def _():
-                    pltpu.make_async_copy(src, dst, recvs.at[10]).start()
-
-                @pl.when(jnp.logical_not(same_core))
-                def _():
-                    send(src, dst, 10, target)
-            else:
-                send(src, dst, 10, target)
+    for dz in A_ORDER_Z:
+        for dp in A_ORDER_P:
+            yp = (chip + dp) % NY
+            target = (y * NZH + (zh + dz) % NZH, yp * 2 + zh // 2)
+            here = same_core if (dp, dz) == (0, 0) else None
+            deliver(ya.at[yp], nua.at[zh % 2, :, place], 10, target, here)
+    took(recvs, 7, zb)
+    for d in Y_ORDER:
+        send(zb, nub.at[:, :, :, y], 9, along_y(d))
+    nub[:, :, :, y] = zb[...]
     took(recvs, 8, mu.at[:, pl.ds(0, 7)])
     half = mu.at[:, pl.ds(k * 8, 8)]
     send(half, half, 11, sibling)
     took(recvs, 11, mu.at[:, pl.ds(0, 8)])
-    took(recvs, 9, nub)
+    took(recvs, 9, nub.at[:, :, :, pl.ds(0, 7)])
     took(recvs, 10, nua)
 
     def dot(left, right):
@@ -179,7 +170,7 @@
     for h in range(2):
         for n in range(2):
             at = pl.ds(n * 8, 8)
-            right = [nua[h, at]] + [nub[h, q, at] for q in range(3)]
+            right = [nua[h, q, at] for q in range(2)] + [nub[h, q, n] for q in range(2)]
             value = dot(left, jnp.concatenate([v.reshape(256, 128) for v in right], axis=1))
             out_ref[:, h * 512 + n * 256 : h * 512 + (n + 1) * 256] = (value * SCALE).astype(BF16)
 
@@ -190,21 +181,22 @@
     took(sends, 4, theirs)
     took(sends, 5, landed.at[pl.ds(0, 7)])
     took(sends, 6, ya.at[pl.ds(0, 7)])
-    took(sends, 7, zb.at[pl.ds(0, 3)])
+    took(sends, 9, nub.at[:, :, :, pl.ds(0, 7)])
     took(sends, 8, mu.at[:, pl.ds(0, 7)])
     took(sends, 11, mu.at[:, pl.ds(0, 8)])
 
-    @pl.when(at_home)
-    def _():
-        took(sends, 9, nub.at[:, :, pl.ds(0, 15)])
-
-    @pl.when(jnp.logical_not(at_home))
-    def _():
-        took(sends, 9, nub)
+    @pl.when(at_home & same_core)
+    def _():
+        took(sends, 7, zb.at[:, :, 0])
+        took(sends, 7, zb.at[0, :, 0])
+
+    @pl.when(jnp.logical_not(at_home & same_core))
+    def _():
+        took(sends, 7, zb)
 
     @pl.when(same_core)
     def _():
-        took(sends, 10, nua.at[0, pl.ds(0, 15)])
+        took(sends, 10, nua.at[0, :, pl.ds(0, 15)])
         took(sends, 10, nua.at[0])
 
     @pl.when(jnp.logical_not(same_core))
@@ -239,10 +231,10 @@
             pltpu.VMEM((8, 32, 512), BF16),
             pltpu.VMEM((4, 32, 128), BF16),
             pltpu.VMEM((4, 16, 32, 128), BF16),
-            pltpu.VMEM((8, 32, 128), BF16),
-            pltpu.VMEM((4, 3, 32, 128), BF16),
-            pltpu.VMEM((2, 16, 32, 128), BF16),
-            pltpu.VMEM((2, 3, 16, 32, 128), BF16),
+            pltpu.VMEM((8, 2, 32, 128), BF16),
+            pltpu.VMEM((2, 2, 2, 32, 128), BF16),
+            pltpu.VMEM((2, 2, 16, 32, 128), BF16),
+            pltpu.VMEM((2, 2, 2, 8, 32, 128), BF16),
             pltpu.SemaphoreType.DMA((12,)),
             pltpu.SemaphoreType.DMA((12,)),
             pltpu.SemaphoreType.DMA((4,)),

time: 63.8 us -> 60 us (0.940); the launches traced: 62.6 us -> 59.8 us
  Pallas kernels: 61.6 us -> 58.8 us
    pallas_call x1, Pallas kernels: 61.6 us -> 58.8 us  [body(): pl.pallas_call(kernel, out_shape=jax.ShapeDtypeStruct((512, 1024), BF16),...]
where the time goes in v3:
time: 60 us; the launch traced here: 59.8 us
  Pallas kernels  58.8 us (98%)
  local copies, waits for them, and re-layouts  0.97 us (2%)
    pallas_call x1, Pallas kernels, body(): pl.pallas_call(kernel, out_shape=jax.ShapeDtypeStruct((512, 1024), BF16),...  58.8 us

profile of v3, /device:TPU:1, one launch (start us, length us, event | category | flops | bytes accessed | tf_op | source)
XLA Modules:
  0.0 59.8 jit_solution(14156740841497429565)
XLA Ops:
  0.0 58.8 %shard_map.46 = bf16[512,1024]{1,0:T(8,128)(2,1)S(1)} custom-call(s32[1,1,8]{2,1,0:T(1,128)} %slot_hbm.1, s32[2,8]{1,0:T(2,128)} %bitcast.3, bf16[32,256]{1,0:T(8,128)(2,1)} %coeff_hbm.1, bf16[8,2,128,128]{3,2,1,0:T(8,128)(2,1)} %bitcast.2), custom_call_target="tpu_custom_call" | custom-call | flops 805306368 | bytes 1638400 | tf_op jit(solution)/shard_map/pallas_call | solution.py:209
  58.8 1.0 %copy.6 = bf16[512,1024]{1,0:T(8,128)(2,1)} copy(bf16[512,1024]{1,0:T(8,128)(2,1)S(1)} %shard_map.46) | data formatting | bytes 2097152

commit v4 on v3

v4 whole, which is shorter than its diff:
```python
import jax
import jax.numpy as jnp
from jax import lax
from jax.experimental import pallas as pl
from jax.experimental.pallas import tpu as pltpu
from jax.sharding import PartitionSpec as P

MESH = pl.DeviceIdType.MESH
BF16 = jnp.bfloat16
F32 = jnp.float32
NY, NZH, NX = 8, 4, 4
Y_ORDER = (4, 3, 5, 2, 6, 1, 7)
Z_ORDER = (2, 1, 3)
A_ORDER_P = (6, 1, 3, 2, 5, 7, 4, 0)
A_ORDER_Z = (2, 1, 3, 0)
SCALE = 512.0**-0.5


def kernel(
    slot_hbm, mask_hbm, coeff_hbm, blocks_hbm, out_ref,
    slot_ref, mask_ref, coeff_ref, blocks,
    ga0, ga1, gb0, gb1, lhs, rhs, part, own, theirs, summed, landed, piece, mu, ya, zb, nua, nub, sends, recvs, local,
):
    row, col = lax.axis_index("row"), lax.axis_index("col")
    ga, gb = (ga0, ga1), (gb0, gb1)
    y, zh = row // NZH, row % NZH
    chip, k = col // 2, col % 2
    zl, x = chip // NX, chip % NX

    def along_y(d):
        return (((y + d) % NY) * NZH + zh, col)

    def along_z(d):
        return (y * NZH + (zh + d) % NZH, col)

    def in_row(d):
        return (row, ((chip + d) % 8) * 2 + k)

    sibling = (row, chip * 2 + 1 - k)

    def send(src, dst, o, index, device):
        pltpu.make_async_remote_copy(
            src_ref=src, dst_ref=dst, send_sem=sends.at[o, index], recv_sem=recvs.at[o, index],
            device_id=device, device_id_type=MESH,
        ).start()

    def took(sems, o, index, ref):
        pltpu.make_async_copy(ref, ref, sems.at[o, index]).wait()

    fetches = [
        pltpu.make_async_copy(src, dst, local.at[n])
        for n, (src, dst) in enumerate(
            ((coeff_hbm, coeff_ref), (slot_hbm, slot_ref), (mask_hbm, mask_ref), (blocks_hbm, blocks))
        )
    ]
    for fetch in fetches:
        fetch.start()
    barrier = pltpu.get_barrier_semaphore()
    peers = [along_y(d) for d in Y_ORDER] + [along_z(d) for d in Z_ORDER] + [in_row(d) for d in range(1, 8)] + [sibling]
    for peer in peers:
        pl.semaphore_signal(barrier, inc=1, device_id=peer, device_id_type=MESH)
    fetches[0].wait()
    for o in range(2):
        ga[o][y, zh] = coeff_ref[0:16, o * 128 : (o + 1) * 128]
        gb[o][zh, y] = coeff_ref[16:32, o * 128 : (o + 1) * 128]
    pl.semaphore_wait(barrier, len(peers))

    for o in range(2):
        for d in Z_ORDER:
            send(ga[o].at[y, zh], ga[o].at[y, zh], o, 0, along_z(d))
        for d in Y_ORDER:
            send(gb[o].at[zh, y], gb[o].at[zh, y], o, 1, along_y(d))
    for fetch in fetches[1:]:
        fetch.wait()
    zero = jnp.zeros((256, 128), BF16)
    for mb in range(4):
        for s in range(8):
            here = (slot_ref[0, 0, s] >> 3) == mb
            lhs[mb, :, s * 128 : (s + 1) * 128] = jnp.where(here, blocks[s].reshape(256, 128), zero)
    for o in range(2):
        took(recvs, o, 0, ga[o].at[0, pl.ds(0, 3)])
        for d in Y_ORDER:
            send(ga[o].at[y], ga[o].at[y], o, 2, along_y(d))
        took(recvs, o, 1, gb[o].at[0, pl.ds(0, 7)])
        for d in Z_ORDER:
            send(gb[o].at[zh], gb[o].at[zh], o, 3, along_z(d))

    def partial(o, first):
        left = lhs[pl.ds(first, 2)].reshape(512, 1024)
        return jnp.dot(left, rhs[o], preferred_element_type=F32).reshape(2, 2, 128, 128)

    def expand(o):
        took(recvs, o, 2, ga[o].at[pl.ds(0, 7)])
        took(recvs, o, 3, gb[o].at[pl.ds(0, 3)])
        for s in range(8):
            nb = slot_ref[0, 0, s] & 7
            rows = jnp.concatenate([ga[o][nb], gb[o][:, nb]], axis=1).reshape(128, 128)
            rhs[o, s * 128 : (s + 1) * 128, :] = jnp.where(mask_ref[o, nb] != 0, rows, jnp.zeros((128, 128), BF16))
        value = partial(o, (1 - k) * 2).astype(BF16)
        for j in range(2):
            for p in range(2):
                part[o, j * 128 : (j + 1) * 128, p * 128 : (p + 1) * 128] = value[j, p]
        send(part.at[o], theirs.at[o], o, 4, sibling)
        value = partial(o, k * 2)
        for j in range(2):
            for p in range(2):
                own[o, j * 128 : (j + 1) * 128, p * 128 : (p + 1) * 128] = value[j, p]
        landed[o, chip] = jnp.zeros((32, 256), BF16)
        took(recvs, o, 4, theirs.at[o])
        total = own[o] + theirs[o].astype(F32)
        own[o] = total
        summed[o] = total.astype(BF16).reshape(8, 32, 256)
        for d in (6, 2, 5, 7, 1, 3, 4):
            send(summed.at[o, (chip + d) % 8], landed.at[o, chip], o, 5, in_row(d))

    place = k * 8 + chip
    at_home, same_core = chip == y, k == zh // 2

    def deliver(src, dst, o, index, device, here):
        if here is None:
            send(src, dst, o, index, device)
            return

        @pl.when(here)
        def _():
            pltpu.make_async_copy(src, dst, recvs.at[o, index]).start()

        @pl.when(jnp.logical_not(here))
        def _():
            send(src, dst, o, index, device)

    def spread(o):
        took(recvs, o, 5, landed.at[o, pl.ds(0, 7)])
        total = own[o, pl.ds(chip * 32, 32), :]
        for m in range(8):
            total = total + landed[o, m].astype(F32)
        total = total.astype(BF16)
        for p in range(2):
            block = total[:, p * 128 : (p + 1) * 128]
            piece[o, p] = block
            mu[o, p, place] = block
        ya[o, y] = total[:, 0:128]
        for dz in (2, 1, 3, 0):
            target = (chip * NZH + (zh + dz) % NZH, y * 2 + zh // 2)
            here = at_home & same_core if dz == 0 else None
            deliver(piece.at[o, 1], zb.at[o, zh % 2, k], o, 7, target, here)
        for d in Y_ORDER:
            send(ya.at[o, y], ya.at[o, y], o, 6, along_y(d))
        for d in (6, 2, 5, 7, 1, 3, 4):
            send(piece.at[o], mu.at[o, :, place], o, 8, in_row(d))

    def within_plane(o):
        took(recvs, o, 6, ya.at[o, pl.ds(0, 7)])
        for dz in A_ORDER_Z:
            for dp in A_ORDER_P:
                yp = (chip + dp) % NY
                target = (y * NZH + (zh + dz) % NZH, yp * 2 + zh // 2)
                here = same_core if (dp, dz) == (0, 0) else None
                deliver(ya.at[o, yp], nua.at[o, zh % 2, place], o, 10, target, here)

    def over_y(o):
        took(recvs, o, 7, zb.at[o])
        for d in Y_ORDER:
            send(zb.at[o], nub.at[o, :, :, y], o, 9, along_y(d))
        nub[o, :, :, y] = zb[o]

    expand(0)
    expand(1)
    spread(0)
    spread(1)
    within_plane(0)
    over_y(0)
    within_plane(1)
    over_y(1)
    for o in range(2):
        took(recvs, o, 8, mu.at[o, :, pl.ds(0, 7)])
        half = mu.at[o, :, pl.ds(k * 8, 8)]
        send(half, half, o, 11, sibling)
    for o in range(2):
        took(recvs, o, 11, mu.at[o, :, pl.ds(0, 8)])
        took(recvs, o, 9, nub.at[o, :, :, pl.ds(0, 7)])
        took(recvs, o, 10, nua.at[o])

    def dot(left, right):
        return lax.dot_general(left, right, (((1,), (1,)), ((), ())), preferred_element_type=F32)

    left = jnp.concatenate([mu[o, p].reshape(512, 128) for o in range(2) for p in range(2)], axis=1)
    for h in range(2):
        for n in range(2):
            right = []
            for o in range(2):
                right += [nua[o, h, pl.ds(n * 8, 8)].reshape(256, 128), nub[o, h, n].reshape(256, 128)]
            value = dot(left, jnp.concatenate(right, axis=1))
            out_ref[:, h * 512 + n * 256 : h * 512 + (n + 1) * 256] = (value * SCALE).astype(BF16)

    for o in range(2):
        took(sends, o, 0, ga[o].at[0, pl.ds(0, 3)])
        took(sends, o, 1, gb[o].at[0, pl.ds(0, 7)])
        took(sends, o, 2, ga[o].at[pl.ds(0, 7)])
        took(sends, o, 3, gb[o].at[pl.ds(0, 3)])
        took(sends, o, 4, theirs.at[o])
        took(sends, o, 5, landed.at[o, pl.ds(0, 7)])
        took(sends, o, 6, ya.at[o, pl.ds(0, 7)])
        took(sends, o, 8, mu.at[o, :, pl.ds(0, 7)])
        took(sends, o, 9, nub.at[o, :, :, pl.ds(0, 7)])
        took(sends, o, 11, mu.at[o, :, pl.ds(0, 8)])

    @pl.when(at_home & same_core)
    def _():
        for o in range(2):
            took(sends, o, 7, zb.at[o, 0])
            took(sends, o, 7, zb.at[o, 0, 0])

    @pl.when(jnp.logical_not(at_home & same_core))
    def _():
        for o in range(2):
            took(sends, o, 7, zb.at[o])

    @pl.when(same_core)
    def _():
        for o in range(2):
            took(sends, o, 10, nua.at[o, 0, pl.ds(0, 15)])
            took(sends, o, 10, nua.at[o, 0])

    @pl.when(jnp.logical_not(same_core))
    def _():
        for o in range(2):
            took(sends, o, 10, nua.at[o])


def body(three_index, slot_pair, coeff, occ_mask):
    arrays = (slot_pair, occ_mask.T, coeff, three_index.reshape(8, 2, 128, 128))
    return pl.pallas_call(
        kernel,
        out_shape=jax.ShapeDtypeStruct((512, 1024), BF16),
        in_specs=[
            pl.BlockSpec(memory_space=pltpu.HBM),
            pl.BlockSpec(memory_space=pltpu.HBM),
            pl.BlockSpec(memory_space=pltpu.HBM),
            pl.BlockSpec(memory_space=pltpu.HBM),
        ],
        out_specs=pl.BlockSpec(memory_space=pltpu.VMEM),
        scratch_shapes=[
            pltpu.SMEM((1, 1, 8), jnp.int32),
            pltpu.SMEM((2, 8), jnp.int32),
            pltpu.VMEM((32, 256), BF16),
            pltpu.VMEM((8, 2, 128, 128), BF16),
            pltpu.VMEM((8, 4, 16, 128), BF16),
            pltpu.VMEM((8, 4, 16, 128), BF16),
            pltpu.VMEM((4, 8, 16, 128), BF16),
            pltpu.VMEM((4, 8, 16, 128), BF16),
            pltpu.VMEM((4, 256, 1024), BF16),
            pltpu.VMEM((2, 1024, 128), BF16),
            pltpu.VMEM((2, 256, 256), BF16),
            pltpu.VMEM((2, 256, 256), F32),
            pltpu.VMEM((2, 256, 256), BF16),
            pltpu.VMEM((2, 8, 32, 256), BF16),
            pltpu.VMEM((2, 8, 32, 256), BF16),
            pltpu.VMEM((2, 2, 32, 128), BF16),
            pltpu.VMEM((2, 2, 16, 32, 128), BF16),
            pltpu.VMEM((2, 8, 32, 128), BF16),
            pltpu.VMEM((2, 2, 2, 32, 128), BF16),
            pltpu.VMEM((2, 2, 16, 32, 128), BF16),
            pltpu.VMEM((2, 2, 2, 8, 32, 128), BF16),
            pltpu.SemaphoreType.DMA((2, 12)),
            pltpu.SemaphoreType.DMA((2, 12)),
            pltpu.SemaphoreType.DMA((4,)),
        ],
        compiler_params=pltpu.CompilerParams(
            collective_id=0, has_side_effects=True, vmem_limit_bytes=40 * 2**20
        ),
        cost_estimate=pl.CostEstimate(flops=805306368, bytes_accessed=1638400, transcendentals=0),
    )(*(pltpu.with_memory_space_constraint(v, pltpu.HBM) for v in arrays))


def solution(mesh):
    return jax.shard_map(
        body,
        mesh=mesh,
        in_specs=(
            P("row", "col", None, None, None, None),
            P("row", "col", None),
            P(("col", "row"), None),
            P("col", None),
        ),
        out_specs=P("row", "col"),
        check_vma=False,
    )
```

time: 60 us -> 59.3 us (0.988)
  Pallas kernels: 58.8 us -> 58.1 us
    pallas_call x1, Pallas kernels: 58.8 us -> 58.1 us  [body(): pl.pallas_call(kernel, out_shape=jax.ShapeDtypeStruct((512, 1024), BF16),...]
where the time goes in v4:
time: 59.3 us; the launch traced here: 59.1 us
  Pallas kernels  58.1 us (98%)
  local copies, waits for them, and re-layouts  0.97 us (2%)
    pallas_call x1, Pallas kernels, body(): pl.pallas_call(kernel, out_shape=jax.ShapeDtypeStruct((512, 1024), BF16),...  58.1 us

profile of v4, /device:TPU:1, one launch (start us, length us, event | category | flops | bytes accessed | tf_op | source)
XLA Modules:
  0.0 59.1 jit_solution(9458756666112454917)
XLA Ops:
  0.0 58.1 %shard_map.46 = bf16[512,1024]{1,0:T(8,128)(2,1)S(1)} custom-call(s32[1,1,8]{2,1,0:T(1,128)} %slot_hbm.1, s32[2,8]{1,0:T(2,128)} %bitcast.3, bf16[32,256]{1,0:T(8,128)(2,1)} %coeff_hbm.1, bf16[8,2,128,128]{3,2,1,0:T(8,128)(2,1)} %bitcast.2), custom_call_target="tpu_custom_call" | custom-call | flops 805306368 | bytes 1638400 | tf_op jit(solution)/shard_map/pallas_call | solution.py:233
  58.1 1.0 %copy.6 = bf16[512,1024]{1,0:T(8,128)(2,1)} copy(bf16[512,1024]{1,0:T(8,128)(2,1)S(1)} %shard_map.46) | data formatting | bytes 2097152

commit v5 on v4

--- a/solution.py
+++ b/solution.py
@@ -11,15 +11,14 @@
 NY, NZH, NX = 8, 4, 4
 Y_ORDER = (4, 3, 5, 2, 6, 1, 7)
 Z_ORDER = (2, 1, 3)
-A_ORDER_P = (6, 1, 3, 2, 5, 7, 4, 0)
-A_ORDER_Z = (2, 1, 3, 0)
+PLANE_ORDER = (0, 1, 7, 2, 6, 3, 5, 4)
 SCALE = 512.0**-0.5
 
 
 def kernel(
     slot_hbm, mask_hbm, coeff_hbm, blocks_hbm, out_ref,
     slot_ref, mask_ref, coeff_ref, blocks,
-    ga0, ga1, gb0, gb1, lhs, rhs, part, own, theirs, summed, landed, piece, mu, ya, zb, nua, nub, sends, recvs, local,
+    ga0, ga1, gb0, gb1, lhs, rhs, part, own, theirs, summed, landed, piece, mu, ya, zb, nua, nub, sends, recvs, from_z, from_y, from_plane, from_b, local,
 ):
     row, col = lax.axis_index("row"), lax.axis_index("col")
     ga, gb = (ga0, ga1), (gb0, gb1)
@@ -36,11 +35,16 @@
     def in_row(d):
         return (row, ((chip + d) % 8) * 2 + k)
 
+    def along_x(d):
+        return (row, (zl * NX + (x + d) % NX) * 2 + k)
+
     sibling = (row, chip * 2 + 1 - k)
-
-    def send(src, dst, o, index, device):
+    across = (1 - zl) * NX + x
+
+    def send(src, dst, o, index, device, arrival=None):
         pltpu.make_async_remote_copy(
-            src_ref=src, dst_ref=dst, send_sem=sends.at[o, index], recv_sem=recvs.at[o, index],
+            src_ref=src, dst_ref=dst, send_sem=sends.at[o, index],
+            recv_sem=recvs.at[o, index] if arrival is None else arrival,
             device_id=device, device_id_type=MESH,
         ).start()
 
@@ -65,11 +69,24 @@
         gb[o][zh, y] = coeff_ref[16:32, o * 128 : (o + 1) * 128]
     pl.semaphore_wait(barrier, len(peers))
 
-    for o in range(2):
+    def pass_along_y(o, piece):
+        for d in Y_ORDER:
+            send(piece, piece, o, 2, along_y(d))
+
+    def pass_along_z(o, piece):
         for d in Z_ORDER:
-            send(ga[o].at[y, zh], ga[o].at[y, zh], o, 0, along_z(d))
+            send(piece, piece, o, 3, along_z(d))
+
+    for o in range(2):
+        mine = ga[o].at[y, zh]
+        for d in Z_ORDER:
+            send(mine, mine, o, 0, along_z(d), from_z.at[o, d - 1])
+        mine = gb[o].at[zh, y]
         for d in Y_ORDER:
-            send(gb[o].at[zh, y], gb[o].at[zh, y], o, 1, along_y(d))
+            send(mine, mine, o, 1, along_y(d), from_y.at[o, d - 1])
+    for o in range(2):
+        pass_along_y(o, ga[o].at[y, zh])
+        pass_along_z(o, gb[o].at[zh, y])
     for fetch in fetches[1:]:
         fetch.wait()
     zero = jnp.zeros((256, 128), BF16)
@@ -78,12 +95,15 @@
             here = (slot_ref[0, 0, s] >> 3) == mb
             lhs[mb, :, s * 128 : (s + 1) * 128] = jnp.where(here, blocks[s].reshape(256, 128), zero)
     for o in range(2):
-        took(recvs, o, 0, ga[o].at[0, pl.ds(0, 3)])
-        for d in Y_ORDER:
-            send(ga[o].at[y], ga[o].at[y], o, 2, along_y(d))
-        took(recvs, o, 1, gb[o].at[0, pl.ds(0, 7)])
-        for d in Z_ORDER:
-            send(gb[o].at[zh], gb[o].at[zh], o, 3, along_z(d))
+        for d in (1, 7, 2, 6, 3, 5, 4):
+            came = gb[o].at[zh, (y - d + NY) % NY]
+            took(from_y, o, d - 1, came)
+            pass_along_z(o, came)
+    for o in range(2):
+        for d in (1, 3, 2):
+            came = ga[o].at[y, (zh - d + NZH) % NZH]
+            took(from_z, o, d - 1, came)
+            pass_along_y(o, came)
 
     def partial(o, first):
         left = lhs[pl.ds(first, 2)].reshape(512, 1024)
@@ -129,7 +149,9 @@
         def _():
             send(src, dst, o, index, device)
 
-    def spread(o):
+    for o in range(2):
+        expand(o)
+    for o in range(2):
         took(recvs, o, 5, landed.at[o, pl.ds(0, 7)])
         total = own[o, pl.ds(chip * 32, 32), :]
         for m in range(8):
@@ -137,60 +159,57 @@
         total = total.astype(BF16)
         for p in range(2):
             block = total[:, p * 128 : (p + 1) * 128]
-            piece[o, p] = block
-            mu[o, p, place] = block
-        ya[o, y] = total[:, 0:128]
+            piece[p, o] = block
+            mu[p, o, place] = block
+        ya[y, o] = total[:, 0:128]
+
+    for dz in (2, 1, 3, 0):
+        target = (chip * NZH + (zh + dz) % NZH, y * 2 + zh // 2)
+        here = at_home & same_core if dz == 0 else None
+        deliver(piece.at[1], zb.at[zh % 2, :, k], 0, 7, target, here)
+    for d in Y_ORDER:
+        send(ya.at[y], ya.at[y], 0, 6, along_y(d), from_plane.at[d - 1])
+    send(piece, mu.at[:, :, place], 0, 12, (row, across * 2 + k))
+    for d in (2, 1, 3):
+        send(piece, mu.at[:, :, place], 0, 8, along_x(d))
+    for d in PLANE_ORDER:
+        yp = (y - d + NY) % NY
+        if d:
+            pltpu.make_async_copy(ya.at[yp], ya.at[yp], from_plane.at[d - 1]).wait()
         for dz in (2, 1, 3, 0):
-            target = (chip * NZH + (zh + dz) % NZH, y * 2 + zh // 2)
-            here = at_home & same_core if dz == 0 else None
-            deliver(piece.at[o, 1], zb.at[o, zh % 2, k], o, 7, target, here)
-        for d in Y_ORDER:
-            send(ya.at[o, y], ya.at[o, y], o, 6, along_y(d))
-        for d in (6, 2, 5, 7, 1, 3, 4):
-            send(piece.at[o], mu.at[o, :, place], o, 8, in_row(d))
-
-    def within_plane(o):
-        took(recvs, o, 6, ya.at[o, pl.ds(0, 7)])
-        for dz in A_ORDER_Z:
-            for dp in A_ORDER_P:
-                yp = (chip + dp) % NY
-                target = (y * NZH + (zh + dz) % NZH, yp * 2 + zh // 2)
-                here = same_core if (dp, dz) == (0, 0) else None
-                deliver(ya.at[o, yp], nua.at[o, zh % 2, place], o, 10, target, here)
-
-    def over_y(o):
-        took(recvs, o, 7, zb.at[o])
-        for d in Y_ORDER:
-            send(zb.at[o], nub.at[o, :, :, y], o, 9, along_y(d))
-        nub[o, :, :, y] = zb[o]
-
-    expand(0)
-    expand(1)
-    spread(0)
-    spread(1)
-    within_plane(0)
-    over_y(0)
-    within_plane(1)
-    over_y(1)
-    for o in range(2):
-        took(recvs, o, 8, mu.at[o, :, pl.ds(0, 7)])
-        half = mu.at[o, :, pl.ds(k * 8, 8)]
-        send(half, half, o, 11, sibling)
-    for o in range(2):
-        took(recvs, o, 11, mu.at[o, :, pl.ds(0, 8)])
-        took(recvs, o, 9, nub.at[o, :, :, pl.ds(0, 7)])
-        took(recvs, o, 10, nua.at[o])
+            target = (y * NZH + (zh + dz) % NZH, yp * 2 + zh // 2)
+            here = (chip == yp) & same_core if dz == 0 else None
+            deliver(ya.at[yp], nua.at[zh % 2, :, place], 0, 10, target, here)
+    took(recvs, 0, 12, mu.at[:, :, 0])
+    came = mu.at[:, :, k * 8 + across]
+    for d in (2, 1, 3):
+        send(came, came, 0, 13, along_x(d))
+    took(recvs, 0, 7, zb)
+    for d in (3, 5, 2, 6, 1, 7):
+        send(zb, nub.at[:, :, :, y], 0, 9, along_y(d), {3: from_b.at[0], 5: from_b.at[1]}.get(d))
+    nub[:, :, :, y] = zb[...]
+    for n, (d, on) in enumerate(((3, 1), (5, 7))):
+        came = nub.at[:, :, :, (y - d + NY) % NY]
+        pltpu.make_async_copy(came, came, from_b.at[n]).wait()
+        came = nub.at[n, :, :, (y - d + NY) % NY]
+        send(came, came, 0, 14, along_y(on))
+    took(recvs, 0, 8, mu.at[:, :, pl.ds(0, 3)])
+    took(recvs, 0, 13, mu.at[:, :, pl.ds(0, 3)])
+    half = mu.at[:, :, pl.ds(k * 8, 8)]
+    send(half, half, 0, 11, sibling)
+    took(recvs, 0, 11, mu.at[:, :, pl.ds(0, 8)])
+    took(recvs, 0, 9, nub.at[:, :, :, pl.ds(0, 4)])
+    took(recvs, 0, 14, nub.at[:, :, :, 0])
+    took(recvs, 0, 10, nua)
 
     def dot(left, right):
         return lax.dot_general(left, right, (((1,), (1,)), ((), ())), preferred_element_type=F32)
 
-    left = jnp.concatenate([mu[o, p].reshape(512, 128) for o in range(2) for p in range(2)], axis=1)
+    left = jnp.concatenate([mu[p, o].reshape(512, 128) for p in range(2) for o in range(2)], axis=1)
     for h in range(2):
         for n in range(2):
-            right = []
-            for o in range(2):
-                right += [nua[o, h, pl.ds(n * 8, 8)].reshape(256, 128), nub[o, h, n].reshape(256, 128)]
-            value = dot(left, jnp.concatenate(right, axis=1))
+            right = [nua[h, o, pl.ds(n * 8, 8)] for o in range(2)] + [nub[h, o, n] for o in range(2)]
+            value = dot(left, jnp.concatenate([v.reshape(256, 128) for v in right], axis=1))
             out_ref[:, h * 512 + n * 256 : h * 512 + (n + 1) * 256] = (value * SCALE).astype(BF16)
 
     for o in range(2):
@@ -200,32 +219,31 @@
         took(sends, o, 3, gb[o].at[pl.ds(0, 3)])
         took(sends, o, 4, theirs.at[o])
         took(sends, o, 5, landed.at[o, pl.ds(0, 7)])
-        took(sends, o, 6, ya.at[o, pl.ds(0, 7)])
-        took(sends, o, 8, mu.at[o, :, pl.ds(0, 7)])
-        took(sends, o, 9, nub.at[o, :, :, pl.ds(0, 7)])
-        took(sends, o, 11, mu.at[o, :, pl.ds(0, 8)])
+    took(sends, 0, 6, ya.at[pl.ds(0, 7)])
+    took(sends, 0, 8, mu.at[:, :, pl.ds(0, 3)])
+    took(sends, 0, 12, mu.at[:, :, 0])
+    took(sends, 0, 13, mu.at[:, :, pl.ds(0, 3)])
+    took(sends, 0, 14, nub.at[:, :, :, 0])
+    took(sends, 0, 9, nub.at[:, :, :, pl.ds(0, 6)])
+    took(sends, 0, 11, mu.at[:, :, pl.ds(0, 8)])
 
     @pl.when(at_home & same_core)
     def _():
-        for o in range(2):
-            took(sends, o, 7, zb.at[o, 0])
-            took(sends, o, 7, zb.at[o, 0, 0])
+        took(sends, 0, 7, zb.at[:, :, 0])
+        took(sends, 0, 7, zb.at[0, :, 0])
 
     @pl.when(jnp.logical_not(at_home & same_core))
     def _():
-        for o in range(2):
-            took(sends, o, 7, zb.at[o])
+        took(sends, 0, 7, zb)
 
     @pl.when(same_core)
     def _():
-        for o in range(2):
-            took(sends, o, 10, nua.at[o, 0, pl.ds(0, 15)])
-            took(sends, o, 10, nua.at[o, 0])
+        took(sends, 0, 10, nua.at[0, :, pl.ds(0, 15)])
+        took(sends, 0, 10, nua.at[0])
 
     @pl.when(jnp.logical_not(same_core))
     def _():
-        for o in range(2):
-            took(sends, o, 10, nua.at[o])
+        took(sends, 0, 10, nua)
 
 
 def body(three_index, slot_pair, coeff, occ_mask):
@@ -258,12 +276,16 @@
             pltpu.VMEM((2, 8, 32, 256), BF16),
             pltpu.VMEM((2, 2, 32, 128), BF16),
             pltpu.VMEM((2, 2, 16, 32, 128), BF16),
-            pltpu.VMEM((2, 8, 32, 128), BF16),
+            pltpu.VMEM((8, 2, 32, 128), BF16),
             pltpu.VMEM((2, 2, 2, 32, 128), BF16),
             pltpu.VMEM((2, 2, 16, 32, 128), BF16),
             pltpu.VMEM((2, 2, 2, 8, 32, 128), BF16),
-            pltpu.SemaphoreType.DMA((2, 12)),
-            pltpu.SemaphoreType.DMA((2, 12)),
+            pltpu.SemaphoreType.DMA((2, 15)),
+            pltpu.SemaphoreType.DMA((2, 15)),
+            pltpu.SemaphoreType.DMA((2, 3)),
+            pltpu.SemaphoreType.DMA((2, 7)),
+            pltpu.SemaphoreType.DMA((7,)),
+            pltpu.SemaphoreType.DMA((2,)),
             pltpu.SemaphoreType.DMA((4,)),
         ],
         compiler_params=pltpu.CompilerParams(

time: 59.3 us -> 58.5 us (0.987)
  Pallas kernels: 58.1 us -> 57.2 us
    pallas_call x1, Pallas kernels: 58.1 us -> 57.2 us  [body(): pl.pallas_call(kernel, out_shape=jax.ShapeDtypeStruct((512, 1024), BF16),...]
where the time goes in v5:
time: 58.5 us; the launch traced here: 58.2 us
  Pallas kernels  57.2 us (98%)
  local copies, waits for them, and re-layouts  0.97 us (2%)
    pallas_call x1, Pallas kernels, body(): pl.pallas_call(kernel, out_shape=jax.ShapeDtypeStruct((512, 1024), BF16),...  57.2 us

profile of v5, /device:TPU:1, one launch (start us, length us, event | category | flops | bytes accessed | tf_op | source)
XLA Modules:
  0.0 58.2 jit_solution(13811332661285530484)
XLA Ops:
  0.0 57.2 %shard_map.46 = bf16[512,1024]{1,0:T(8,128)(2,1)S(1)} custom-call(s32[1,1,8]{2,1,0:T(1,128)} %slot_hbm.1, s32[2,8]{1,0:T(2,128)} %bitcast.3, bf16[32,256]{1,0:T(8,128)(2,1)} %coeff_hbm.1, bf16[8,2,128,128]{3,2,1,0:T(8,128)(2,1)} %bitcast.2), custom_call_target="tpu_custom_call" | custom-call | flops 805306368 | bytes 1638400 | tf_op jit(solution)/shard_map/pallas_call | solution.py:251
  57.2 1.0 %copy.6 = bf16[512,1024]{1,0:T(8,128)(2,1)} copy(bf16[512,1024]{1,0:T(8,128)(2,1)S(1)} %shard_map.46) | data formatting | bytes 2097152

commit v6 on v5

--- a/solution.py
+++ b/solution.py
@@ -176,7 +176,7 @@
         yp = (y - d + NY) % NY
         if d:
             pltpu.make_async_copy(ya.at[yp], ya.at[yp], from_plane.at[d - 1]).wait()
-        for dz in (2, 1, 3, 0):
+        for dz in (1, 3, 0, 2):
             target = (y * NZH + (zh + dz) % NZH, yp * 2 + zh // 2)
             here = (chip == yp) & same_core if dz == 0 else None
             deliver(ya.at[yp], nua.at[zh % 2, :, place], 0, 10, target, here)
@@ -185,7 +185,7 @@
     for d in (2, 1, 3):
         send(came, came, 0, 13, along_x(d))
     took(recvs, 0, 7, zb)
-    for d in (3, 5, 2, 6, 1, 7):
+    for d in (3, 5, 1, 7, 2, 6):
         send(zb, nub.at[:, :, :, y], 0, 9, along_y(d), {3: from_b.at[0], 5: from_b.at[1]}.get(d))
     nub[:, :, :, y] = zb[...]
     for n, (d, on) in enumerate(((3, 1), (5, 7))):

time: 58.5 us -> 57.7 us (0.986)
  Pallas kernels: 57.2 us -> 56.5 us
    pallas_call x1, Pallas kernels: 57.2 us -> 56.5 us  [body(): pl.pallas_call(kernel, out_shape=jax.ShapeDtypeStruct((512, 1024), BF16),...]
where the time goes in v6:
time: 57.7 us; the launch traced here: 57.5 us
  Pallas kernels  56.5 us (98%)
  local copies, waits for them, and re-layouts  0.97 us (2%)
    pallas_call x1, Pallas kernels, body(): pl.pallas_call(kernel, out_shape=jax.ShapeDtypeStruct((512, 1024), BF16),...  56.5 us

profile of v6, /device:TPU:1, one launch (start us, length us, event | category | flops | bytes accessed | tf_op | source)
XLA Modules:
  0.0 57.5 jit_solution(16002881999263423948)
XLA Ops:
  0.0 56.5 %shard_map.46 = bf16[512,1024]{1,0:T(8,128)(2,1)S(1)} custom-call(s32[1,1,8]{2,1,0:T(1,128)} %slot_hbm.1, s32[2,8]{1,0:T(2,128)} %bitcast.3, bf16[32,256]{1,0:T(8,128)(2,1)} %coeff_hbm.1, bf16[8,2,128,128]{3,2,1,0:T(8,128)(2,1)} %bitcast.2), custom_call_target="tpu_custom_call" | custom-call | flops 805306368 | bytes 1638400 | tf_op jit(solution)/shard_map/pallas_call | solution.py:251
  56.5 1.0 %copy.6 = bf16[512,1024]{1,0:T(8,128)(2,1)} copy(bf16[512,1024]{1,0:T(8,128)(2,1)S(1)} %shard_map.46) | data formatting | bytes 2097152

commit v7 on v6

--- a/solution.py
+++ b/solution.py
@@ -18,7 +18,7 @@
 def kernel(
     slot_hbm, mask_hbm, coeff_hbm, blocks_hbm, out_ref,
     slot_ref, mask_ref, coeff_ref, blocks,
-    ga0, ga1, gb0, gb1, lhs, rhs, part, own, theirs, summed, landed, piece, mu, ya, zb, nua, nub, sends, recvs, from_z, from_y, from_plane, from_b, local,
+    ga0, ga1, gb0, gb1, lhs, rhs, part, own, theirs, summed, landed, piece, mu, ya, zb, nua, nub, early, sends, recvs, from_z, from_y, from_plane, from_b, local,
 ):
     row, col = lax.axis_index("row"), lax.axis_index("col")
     ga, gb = (ga0, ga1), (gb0, gb1)
@@ -200,16 +200,22 @@
     took(recvs, 0, 11, mu.at[:, :, pl.ds(0, 8)])
     took(recvs, 0, 9, nub.at[:, :, :, pl.ds(0, 4)])
     took(recvs, 0, 14, nub.at[:, :, :, 0])
-    took(recvs, 0, 10, nua)
 
     def dot(left, right):
         return lax.dot_general(left, right, (((1,), (1,)), ((), ())), preferred_element_type=F32)
 
-    left = jnp.concatenate([mu[p, o].reshape(512, 128) for p in range(2) for o in range(2)], axis=1)
+    def left(p):
+        return jnp.concatenate([mu[p, o].reshape(512, 128) for o in range(2)], axis=1)
+
     for h in range(2):
         for n in range(2):
-            right = [nua[h, o, pl.ds(n * 8, 8)] for o in range(2)] + [nub[h, o, n] for o in range(2)]
-            value = dot(left, jnp.concatenate([v.reshape(256, 128) for v in right], axis=1))
+            right = jnp.concatenate([nub[h, o, n].reshape(256, 128) for o in range(2)], axis=1)
+            early[h, n] = dot(left(1), right)
+    took(recvs, 0, 10, nua)
+    for h in range(2):
+        for n in range(2):
+            right = [nua[h, o, pl.ds(n * 8, 8)].reshape(256, 128) for o in range(2)]
+            value = early[h, n] + dot(left(0), jnp.concatenate(right, axis=1))
             out_ref[:, h * 512 + n * 256 : h * 512 + (n + 1) * 256] = (value * SCALE).astype(BF16)
 
     for o in range(2):
@@ -280,6 +286,7 @@
             pltpu.VMEM((2, 2, 2, 32, 128), BF16),
             pltpu.VMEM((2, 2, 16, 32, 128), BF16),
             pltpu.VMEM((2, 2, 2, 8, 32, 128), BF16),
+            pltpu.VMEM((2, 2, 512, 256), F32),
             pltpu.SemaphoreType.DMA((2, 15)),
             pltpu.SemaphoreType.DMA((2, 15)),
             pltpu.SemaphoreType.DMA((2, 3)),

time: 57.7 us -> 57.9 us (level)
  no operation moved by 1% of the time
where the time goes in v7:
time: 57.9 us; the launch traced here: 57.6 us
  Pallas kernels  56.6 us (98%)
  local copies, waits for them, and re-layouts  0.97 us (2%)
    pallas_call x1, Pallas kernels, body(): pl.pallas_call(kernel, out_shape=jax.ShapeDtypeStruct((512, 1024), BF16),...  56.6 us

profile of v7, /device:TPU:1, one launch (start us, length us, event | category | flops | bytes accessed | tf_op | source)
XLA Modules:
  0.0 57.6 jit_solution(16313793460107590038)
XLA Ops:
  0.0 56.6 %shard_map.46 = bf16[512,1024]{1,0:T(8,128)(2,1)S(1)} custom-call(s32[1,1,8]{2,1,0:T(1,128)} %slot_hbm.1, s32[2,8]{1,0:T(2,128)} %bitcast.3, bf16[32,256]{1,0:T(8,128)(2,1)} %coeff_hbm.1, bf16[8,2,128,128]{3,2,1,0:T(8,128)(2,1)} %bitcast.2), custom_call_target="tpu_custom_call" | custom-call | flops 805306368 | bytes 1638400 | tf_op jit(solution)/shard_map/pallas_call | solution.py:257
  56.6 1.0 %copy.6 = bf16[512,1024]{1,0:T(8,128)(2,1)} copy(bf16[512,1024]{1,0:T(8,128)(2,1)S(1)} %shard_map.46) | data formatting | bytes 2097152
